TPU v7x, 32 devices: a whole 2x2x4 slice. The times are simulated.
32 devices in a mesh: segment: 16 (over z, x, core), fsdp: 2 (over y).
Axes of the slice: x: 2, y: 2, z: 4, core: 2. Of those that a mesh axis runs over, the one named last changes fastest.
Arguments:
- stream: bfloat16 [2, 16, 128, 4096], P(None, 'segment', 'fsdp'), may hold values from -60 to 60
- gain: bfloat16 [2, 16, 4096], P(None, 'segment'), may hold values from 0.099609375 to 1.8984375
- w_query: bfloat16 [2, 16, 32, 128, 128], P(None, 'segment', 'fsdp'), may hold values from -20 to 20
- w_key: bfloat16 [2, 16, 32, 128, 128], P(None, 'segment', 'fsdp'), may hold values from -20 to 20
- w_value: bfloat16 [2, 16, 32, 128, 128], P(None, 'segment', 'fsdp'), may hold values from -0.5 to 0.5
- w_mix: bfloat16 [2, 16, 128, 32, 32], P(None, 'segment', 'fsdp'), may hold values from -1 to 1
- active: int32 [2, 16], P(None, 'segment'), may hold values from 0 to 1
- random_blocks: int32 [2, 16, 2, 2], P(None, 'segment'), may hold values from 0 to 1
Outputs:
- advanced: bfloat16 [2, 16, 128, 4096], P(None, 'segment', 'fsdp')
All inputs are finite; a program needn't handle non-finite values.
Results may differ from a plain program's by a relative error of at most 0.009.
Values may be sent and summed in bfloat16 or wider, within the bound.
A program may use at most 64 MiB of HBM per device.

v0:
```python
import jax
import jax.numpy as jnp
from jax import lax
from jax.sharding import PartitionSpec as P

BLK = 64
ROUNDS = 2


EPS = 1e-05


def shifted(value, axis, by):
    devices = lax.axis_size(axis)
    return lax.ppermute(value, axis, [(i, (i + by) % devices) for i in range(devices)])


def block_attention(query, keys, values, random_ids):
    heads, seq_len, head_width = query.shape
    count = seq_len // BLK
    query_blocks = query.reshape(heads, count, BLK, head_width)
    key_blocks = keys.reshape(heads, count, BLK, head_width)
    value_blocks = values.reshape(heads, count, BLK, head_width)
    block_ids = jnp.arange(count, dtype=jnp.int32)
    window = jnp.stack(
        [(block_ids - 1) % count, block_ids, (block_ids + 1) % count, jnp.zeros_like(block_ids)],
        axis=1,
    )
    chosen = jnp.concatenate([window, random_ids], axis=1)
    picked_keys = key_blocks[:, chosen].reshape(heads, count, chosen.shape[1] * BLK, head_width)
    picked_values = value_blocks[:, chosen].reshape(heads, count, chosen.shape[1] * BLK, head_width)
    scores = jnp.einsum(
        "hnqd,hnkd->hnqk", query_blocks, picked_keys, preferred_element_type=jnp.float32
    )
    row_max = jnp.max(scores, axis=-1, keepdims=True)
    powers = jnp.exp(scores - row_max)
    weights = (powers / jnp.sum(powers, axis=-1, keepdims=True)).astype(jnp.bfloat16)
    mixed = jnp.einsum(
        "hnqk,hnkd->hnqd", weights, picked_values, preferred_element_type=jnp.float32
    ).astype(jnp.bfloat16)
    return mixed.reshape(heads, seq_len, head_width)


def head_attention(view, queries_w, keys_w, values_w, random_ids):

    def one_segment(items):
        rows, weight_q, weight_k, weight_v, ids = items
        raw = jnp.einsum("thc,hcd->htd", rows, weight_q, preferred_element_type=jnp.float32)
        query = (raw * rows.shape[-1] ** (-0.5)).astype(jnp.bfloat16)
        keys = jnp.einsum(
            "thc,hcd->htd", rows, weight_k, preferred_element_type=jnp.float32
        ).astype(jnp.bfloat16)
        values = jnp.einsum(
            "thc,hcd->htd", rows, weight_v, preferred_element_type=jnp.float32
        ).astype(jnp.bfloat16)
        return block_attention(query, keys, values, ids)

    return lax.map(one_segment, (view, queries_w, keys_w, values_w, random_ids))


def mix_heads(attended, mix_w):
    return jnp.einsum(
        "vhtc,vchg->vtgc",
        attended,
        lax.all_gather(mix_w, "fsdp", axis=1, tiled=True),
        preferred_element_type=jnp.float32,
    ).astype(jnp.bfloat16)


def cycle(values):
    moved = shifted(values, "segment", 1)
    return jnp.where(lax.axis_index("segment") == 0, jnp.roll(moved, 1, axis=0), moved)


def token_layer(state, params):
    queries_w, keys_w, values_w, mix_w, gains, live, random_ids = params
    wide = state.astype(jnp.float32)
    mean_sq = jnp.mean(wide * wide, axis=2, keepdims=True)
    normed = (wide * lax.rsqrt(mean_sq + EPS) * gains[:, None, :].astype(jnp.float32)).astype(
        jnp.bfloat16
    )
    view = normed.reshape(state.shape[0], state.shape[1], -1, queries_w.shape[-1])
    gathered = lax.all_to_all(view, "fsdp", split_axis=2, concat_axis=1, tiled=True)
    attended = head_attention(gathered, queries_w, keys_w, values_w, random_ids)
    returned = lax.all_to_all(attended, "fsdp", split_axis=2, concat_axis=1, tiled=True)
    mixed = mix_heads(returned, mix_w)
    updated = (wide + mixed.reshape(wide.shape).astype(jnp.float32)).astype(jnp.bfloat16)
    return jnp.where(live[:, None, None] > 0, updated, state)


def shards(stream, gain, w_query, w_key, w_value, w_mix, active, random_blocks):
    params = (
        w_query[:, 0],
        w_key[:, 0],
        w_value[:, 0],
        w_mix[:, 0],
        gain[:, 0],
        active[:, 0],
        random_blocks[:, 0],
    )
    state = stream[:, 0]
    for round_index in range(ROUNDS):
        state = token_layer(state, params)
        state = cycle(state)
    return state[:, None]


def solution(mesh):
    in_specs = (
        P(None, "segment", "fsdp", None),
        P(None, "segment", None),
        P(None, "segment", "fsdp", None, None),
        P(None, "segment", "fsdp", None, None),
        P(None, "segment", "fsdp", None, None),
        P(None, "segment", "fsdp", None, None),
        P(None, "segment"),
        P(None, "segment", None, None),
    )
    out_specs = P(None, "segment", "fsdp", None)
    return jax.shard_map(shards, mesh=mesh, in_specs=in_specs, out_specs=out_specs, check_vma=False)
```

profile of v0, /device:TPU:0, one launch (start us, length us, event | category | flops | bytes accessed | tf_op | source)
XLA Modules:
  0.0 284.1 jit_solution(17027938386886022296)
XLA Ops:
  5.5 4.4 %all-to-all-start = ((bf16[2,64,32,128]{3,1,0,2:T(8,128)(2,1)}), bf16[2,64,32,128]{3,1,0,2:T(8,128)(2,1)S(1)}, u32[]{:S(2)}, u32[]{:S(2)}) async-start(bf16[2,64,32,128]{3,1,0,2:T(8,128)(2,1)} %copy.83), calls=%async_computation | async-start | bytes 2097152 | tf_op jit(solution)/shard_map/all_to_all | solution.py:83
  9.9 14.4 %all-to-all-done = bf16[2,64,32,128]{3,1,0,2:T(8,128)(2,1)S(1)} async-done(((bf16[2,64,32,128]{3,1,0,2:T(8,128)(2,1)}), bf16[2,64,32,128]{3,1,0,2:T(8,128)(2,1)S(1)}, u32[]{:S(2)}, u32[]{:S(2)}) %all-to-all-start) | async-done | bytes 1048608 | tf_op jit(solution)/shard_map/all_to_all | solution.py:83
  27.1 58.8 %while.24 = (s32[]{:T(128)}, bf16[2,16,128,128]{3,1,0,2:T(8,128)(2,1)}, bf16[2,128,16,128]{3,2,1,0:T(8,128)(2,1)}, bf16[2,16,128,128]{3,2,1,0:T(8,128)(2,1)}, bf...) while((s32[]{:T(128)}, ...), condition=%wide.region_4.5_spmd, body=%wide.region_1.4_spmd.sunk | while | flops 609226560 | bytes 61364884 | solution.py:58
  32.6 2.9 %copy.135 = bf16[2,6,16,64,128]{4,3,1,0,2:T(8,128)(2,1)S(1)} copy(bf16[2,6,16,64,128]{4,3,2,1,0:T(8,128)(2,1)} %bitcast.246) | data formatting | bytes 6291456 | tf_op jit(solution)/shard_map/while/body/eval_jaxpr/gather | solution.py:30
  47.0 7.3 %fusion.127 = bf16[16,2,64,128]{3,2,1,0:T(8,128)(2,1)} fusion(bf16[16,2,384,128]{3,2,1,0:T(8,128)(2,1)S(1)} %bitcast.248, f32[16,2,64]{2,1,0:T(2,128)S(1)} %fusion.126, f32[16,2,64,384]{3,2,1,0:T(8,128)} %copy-done), kind=kOutput, calls=%fused_computation.9.clone.1 | convolution fusion | flops 203950464 | bytes 6823936 | tf_op jit(solution)/shard_map/while/body/eval_jaxpr/hnqk,hnkd->hnqd/dot_general | solution.py:38
  62.1 2.9 %copy.135 = bf16[2,6,16,64,128]{4,3,1,0,2:T(8,128)(2,1)S(1)} copy(bf16[2,6,16,64,128]{4,3,2,1,0:T(8,128)(2,1)} %bitcast.246) | data formatting | bytes 6291456 | tf_op jit(solution)/shard_map/while/body/eval_jaxpr/gather | solution.py:30
  76.4 7.3 %fusion.127 = bf16[16,2,64,128]{3,2,1,0:T(8,128)(2,1)} fusion(bf16[16,2,384,128]{3,2,1,0:T(8,128)(2,1)S(1)} %bitcast.248, f32[16,2,64]{2,1,0:T(2,128)S(1)} %fusion.126, f32[16,2,64,384]{3,2,1,0:T(8,128)} %copy-done), kind=kOutput, calls=%fused_computation.9.clone.1 | convolution fusion | flops 203950464 | bytes 6823936 | tf_op jit(solution)/shard_map/while/body/eval_jaxpr/hnqk,hnkd->hnqd/dot_general | solution.py:38
  85.9 3.9 %all-to-all-start.1 = ((bf16[2,16,128,128]{3,1,0,2:T(8,128)(2,1)}), bf16[2,16,128,128]{3,1,0,2:T(8,128)(2,1)S(1)}, u32[]{:S(2)}, u32[]{:S(2)}) async-start(bf16[2,16,128,128]{3,1,0,2:T(8,128)(2,1)} %get-tuple-element.187), calls=%async_computation.1 | async-start | bytes 2097152 | tf_op jit(solution)/shard_map/all_to_all | solution.py:85
  89.8 3.7 %copy.89 = bf16[2,1,64,32,32]{3,4,2,0,1:T(8,128)(2,1)} copy(bf16[2,1,64,32,32]{2,4,3,1,0:T(8,128)(2,1)} %param.17) | data formatting | bytes 524288 | tf_op args[5]
  93.5 31.9 %all-gather = bf16[2,1,128,32,32]{3,4,2,0,1:T(8,128)(2,1)S(1)} all-gather(bf16[2,1,64,32,32]{3,4,2,0,1:T(8,128)(2,1)} %copy.89), channel_id=2, replica_groups=mesh['segment'=16,'fsdp'=2] {'fsdp'}, dimensions={2}, use_global_device_ids=true | all-gather | bytes 786432 | tf_op jit(solution)/shard_map/all_gather | solution.py:65
  125.5 4.1 %copy.88 = bf16[2,16,2,64,128]{3,1,2,4,0:T(8,128)(2,1)} copy(bf16[2,16,2,64,128]{4,1,0,3,2:T(8,128)(2,1)S(1)} %bitcast.258) | data formatting | bytes 2097152 | tf_op jit(solution)/shard_map/all_to_all | solution.py:85
  129.5 4.2 %convert_bitcast_fusion.1 = f32[2,64,32,128]{1,2,3,0:T(8,128)} fusion(bf16[2,32,64,128]{2,1,3,0:T(8,128)(2,1)} %bitcast.257, bf16[2,1,128,32,32]{3,4,2,0,1:T(8,128)(2,1)S(1)} %all-gather), kind=kOutput, calls=%fused_computation.81 | convolution fusion | flops 34603008 | bytes 3670016 | tf_op jit(solution)/shard_map/vhtc,vchg->vtgc/dot_general | solution.py:62
  133.7 5.3 %copy.90 = f32[2,64,32,128]{3,2,1,0:T(8,128)} copy(f32[2,64,32,128]{1,2,3,0:T(8,128)} %convert_bitcast_fusion.1) | data formatting | bytes 4194304 | tf_op jit(solution)/shard_map/convert_element_type | solution.py:87
  142.3 17.1 %collective-permute-done = bf16[2,64,4096]{2,1,0:T(8,128)(2,1)S(1)} collective-permute-done((bf16[2,64,4096]{2,1,0:T(8,128)(2,1)}, bf16[2,64,4096]{2,1,0:T(8,128)(2,1)S(1)}, u32[]{:S(2)}, u32[]{:S(2)}) %collective-permute-start) | collective-permute-done | bytes 1048608 | tf_op jit(solution)/shard_map/ppermute | solution.py:15
  162.3 3.8 %all-to-all-start.2 = ((bf16[2,64,32,128]{3,1,0,2:T(8,128)(2,1)}), bf16[2,64,32,128]{3,1,0,2:T(8,128)(2,1)S(1)}, u32[]{:S(2)}, u32[]{:S(2)}) async-start(bf16[2,64,32,128]{3,1,0,2:T(8,128)(2,1)} %copy_bitcast_fusion.4), calls=%async_computation.2 | async-start | bytes 2097152 | tf_op jit(solution)/shard_map/all_to_all | solution.py:83
  166.1 10.2 %all-to-all-done.2 = bf16[2,64,32,128]{3,1,0,2:T(8,128)(2,1)S(1)} async-done(((bf16[2,64,32,128]{3,1,0,2:T(8,128)(2,1)}), bf16[2,64,32,128]{3,1,0,2:T(8,128)(2,1)S(1)}, u32[]{:S(2)}, u32[]{:S(2)}) %all-to-all-start.2) | async-done | bytes 1048608 | tf_op jit(solution)/shard_map/all_to_all | solution.py:83
  178.6 57.7 %while.25 = (s32[]{:T(128)}, bf16[2,16,128,128]{3,1,0,2:T(8,128)(2,1)}, bf16[2,128,16,128]{3,1,2,0:T(8,128)(2,1)}, bf16[2,16,128,128]{3,2,1,0:T(8,128)(2,1)}, bf...) while((s32[]{:T(128)}, ...), condition=%wide.region_9.10_spmd, body=%wide.region_6.9_spmd.sunk | while | flops 609226560 | bytes 60317840 | solution.py:58
  197.9 7.3 %fusion.144 = bf16[16,2,64,128]{3,2,1,0:T(8,128)(2,1)} fusion(bf16[16,2,384,128]{3,2,1,0:T(8,128)(2,1)S(1)} %bitcast.249, f32[16,2,64]{2,1,0:T(2,128)S(1)} %fusion.143, f32[16,2,64,384]{3,2,1,0:T(8,128)} %copy-done.1), kind=kOutput, calls=%fused_computation.45.clone.1 | convolution fusion | flops 203950464 | bytes 6823936 | tf_op jit(solution)/shard_map/while/body/eval_jaxpr/hnqk,hnkd->hnqd/dot_general | solution.py:38
  226.8 7.3 %fusion.144 = bf16[16,2,64,128]{3,2,1,0:T(8,128)(2,1)} fusion(bf16[16,2,384,128]{3,2,1,0:T(8,128)(2,1)S(1)} %bitcast.249, f32[16,2,64]{2,1,0:T(2,128)S(1)} %fusion.143, f32[16,2,64,384]{3,2,1,0:T(8,128)} %copy-done.1), kind=kOutput, calls=%fused_computation.45.clone.1 | convolution fusion | flops 203950464 | bytes 6823936 | tf_op jit(solution)/shard_map/while/body/eval_jaxpr/hnqk,hnkd->hnqd/dot_general | solution.py:38
  236.3 13.2 %all_to_all.72 = bf16[2,16,128,128]{3,1,0,2:T(8,128)(2,1)S(1)} all-to-all(bf16[2,16,128,128]{3,1,0,2:T(8,128)(2,1)} %get-tuple-element.188), channel_id=1, replica_groups=mesh['segment'=16,'fsdp'=2] {'fsdp'}, dimensions={2} | all-to-all | bytes 2097152 | tf_op jit(solution)/shard_map/all_to_all | solution.py:85
  249.6 4.1 %copy.94 = bf16[2,16,2,64,128]{3,1,2,4,0:T(8,128)(2,1)} copy(bf16[2,16,2,64,128]{4,1,0,3,2:T(8,128)(2,1)S(1)} %bitcast.259) | data formatting | bytes 2097152 | tf_op jit(solution)/shard_map/all_to_all | solution.py:85
  253.6 4.2 %convert_bitcast_fusion = f32[2,64,32,128]{1,2,3,0:T(8,128)} fusion(bf16[2,32,64,128]{2,1,3,0:T(8,128)(2,1)} %bitcast.256, bf16[2,1,128,32,32]{3,4,2,0,1:T(8,128)(2,1)S(1)} %copy-done.3), kind=kOutput, calls=%fused_computation.80 | convolution fusion | flops 34603008 | bytes 3670016 | tf_op jit(solution)/shard_map/vhtc,vchg->vtgc/dot_general | solution.py:62
  257.8 4.5 %copy.95 = f32[2,64,32,128]{3,2,1,0:T(8,128)S(1)} copy(f32[2,64,32,128]{1,2,3,0:T(8,128)} %convert_bitcast_fusion) | data formatting | bytes 4194304 | tf_op jit(solution)/shard_map/convert_element_type | solution.py:87
  266.0 16.9 %collective-permute-done.1 = bf16[2,64,4096]{2,1,0:T(8,128)(2,1)S(1)} collective-permute-done((bf16[2,64,4096]{2,1,0:T(8,128)(2,1)S(1)}, bf16[2,64,4096]{2,1,0:T(8,128)(2,1)S(1)}, u32[]{:S(2)}, u32[]{:S(2)}) %collective-permute-start.1) | collective-permute-done | bytes 1048608 | tf_op jit(solution)/shard_map/ppermute | solution.py:15
  (127 shorter events, 102.7 us)
Async XLA Ops:
  5.5 21.6 %copy-start.7 = (s32[2,1,2,2]{3,2,1,0:T(2,128)S(1)}, s32[2,1,2,2]{3,2,1,0:T(2,128)}, u32[]{:S(2)}) copy-start(s32[2,1,2,2]{3,2,1,0:T(2,128)} %param.19) | copy-start | bytes 100
  5.5 18.8 %all-to-all-start = ((bf16[2,64,32,128]{3,1,0,2:T(8,128)(2,1)}), bf16[2,64,32,128]{3,1,0,2:T(8,128)(2,1)S(1)}, u32[]{:S(2)}, u32[]{:S(2)}) async-start(bf16[2,64,32,128]{3,1,0,2:T(8,128)(2,1)} %copy.83), calls=%async_computation | async-start | bytes 2097152 | tf_op jit(solution)/shard_map/all_to_all | solution.py:83
  38.4 1.7 copy-start
  67.8 1.7 copy-start
  85.9 39.5 %copy-start.8 = (s32[2,1]{0,1:T(1,128)S(1)}, s32[2,1]{0,1:T(1,128)}, u32[]{:S(2)}) copy-start(s32[2,1]{0,1:T(1,128)} %param.18) | copy-start | bytes 28
  85.9 39.5 %all-to-all-start.1 = ((bf16[2,16,128,128]{3,1,0,2:T(8,128)(2,1)}), bf16[2,16,128,128]{3,1,0,2:T(8,128)(2,1)S(1)}, u32[]{:S(2)}, u32[]{:S(2)}) async-start(bf16[2,16,128,128]{3,1,0,2:T(8,128)(2,1)} %get-tuple-element.187), calls=%async_computation.1 | async-start | bytes 2097152 | tf_op jit(solution)/shard_map/all_to_all | solution.py:85
  125.4 8.3 %copy-start.2 = (bf16[2,1,128,32,32]{3,4,2,0,1:T(8,128)(2,1)}, bf16[2,1,128,32,32]{3,4,2,0,1:T(8,128)(2,1)S(1)}, u32[]{:S(2)}) copy-start(bf16[2,1,128,32,32]{3,4,2,0,1:T(8,128)(2,1)S(1)} %all-gather) | copy-start | bytes 1572868
  139.0 1.9 copy-start.4
  142.3 17.1 %collective-permute-start = (bf16[2,64,4096]{2,1,0:T(8,128)(2,1)}, bf16[2,64,4096]{2,1,0:T(8,128)(2,1)S(1)}, u32[]{:S(2)}, u32[]{:S(2)}) collective-permute-start(bf16[2,64,4096]{2,1,0:T(8,128)(2,1)} %fusion.61), channel_id=1, source_target_pairs={{0,2},{2,4},{4,6},{6,8},{8,10},{10,12},{12,14},{14,16},{16,18},{18... | collective-permute-start | bytes 3145736 | tf_op jit(solution)/shard_map/ppermute | solution.py:15
  160.0 1.0 copy-start.5
  162.3 14.0 %all-to-all-start.2 = ((bf16[2,64,32,128]{3,1,0,2:T(8,128)(2,1)}), bf16[2,64,32,128]{3,1,0,2:T(8,128)(2,1)S(1)}, u32[]{:S(2)}, u32[]{:S(2)}) async-start(bf16[2,64,32,128]{3,1,0,2:T(8,128)(2,1)} %copy_bitcast_fusion.4), calls=%async_computation.2 | async-start | bytes 2097152 | tf_op jit(solution)/shard_map/all_to_all | solution.py:83
  189.2 1.7 copy-start.1
  218.0 1.7 copy-start.1
  236.3 17.3 %copy-start.3 = (bf16[2,1,128,32,32]{3,4,2,0,1:T(8,128)(2,1)S(1)}, bf16[2,1,128,32,32]{3,4,2,0,1:T(8,128)(2,1)}, u32[]{:S(2)}) copy-start(bf16[2,1,128,32,32]{3,4,2,0,1:T(8,128)(2,1)} %copy-done.2) | copy-start | bytes 1572868
  262.3 1.6 copy-start.6
  265.9 17.0 %collective-permute-start.1 = (bf16[2,64,4096]{2,1,0:T(8,128)(2,1)S(1)}, bf16[2,64,4096]{2,1,0:T(8,128)(2,1)S(1)}, u32[]{:S(2)}, u32[]{:S(2)}) collective-permute-start(bf16[2,64,4096]{2,1,0:T(8,128)(2,1)S(1)} %fusion.60), channel_id=1, source_target_pairs={{0,2},{2,4},{4,6},{6,8},{8,10},{10,12},{12,14},{14,16},{16,18},{18... | collective-permute-start | bytes 3145736 | tf_op jit(solution)/shard_map/ppermute | solution.py:15
where the time goes:
time: 286 us; the launch traced here: 284 us
  local copies, waits for them, and re-layouts  91.9 us (32%)
  matrix products  60.7 us (21%)
  waiting for transfers between devices  58.7 us (21%)
  blocking collectives  45.2 us (16%)
  other arithmetic  15 us (5%)
  starting transfers between devices  12.1 us (4%)
    ppermute x2, waiting for transfers between devices, shifted(): lax.ppermute(value, axis, [(i, (i + by) % devices) for i in range(devices)])  34 us
    all_gather x1, blocking collectives, mix_heads(): lax.all_gather(mix_w, 'fsdp', axis=1, tiled=True)  31.9 us
    dot_general x4, matrix products, block_attention(): jnp.einsum('hnqk,hnkd->hnqd', weights, picked_values, preferred_element_t...  29.3 us
    all_to_all x2, waiting for transfers between devices, token_layer(): lax.all_to_all(view, 'fsdp', split_axis=2, concat_axis=1, tiled=True)  24.7 us
    gather x8, local copies, waits for them, and re-layouts, block_attention(): value_blocks[:, chosen]  22.4 us
    gather x8, local copies, waits for them, and re-layouts, block_attention(): key_blocks[:, chosen]  22.4 us
    all_to_all x1, blocking collectives, token_layer(): lax.all_to_all(attended, 'fsdp', split_axis=2, concat_axis=1, tiled=True)  13.2 us
    convert_element_type x4, local copies, waits for them, and re-layouts, token_layer(): mixed.reshape(wide.shape).astype(jnp.float32)  13.2 us
  transfers between devices with their start and end apart: 5, of which 4 were waited for; matrix products, arithmetic and copies ran while one was open for 1% of the time, Pallas kernels for 0%

commit v1 on v0

v1 whole, which is shorter than its diff:
```python
import functools

import jax
import jax.numpy as jnp
from jax import lax
from jax.experimental import pallas as pl
from jax.experimental.pallas import tpu as pltpu
from jax.sharding import PartitionSpec as P

BLK = 64
ROUNDS = 2
EPS = 1e-05
LANES = 128
MESH = pl.DeviceIdType.MESH
F32 = jnp.float32
BF16 = jnp.bfloat16


def kernel(
    segments, peers, stream, gain, wq, wk, wv, wm, live, ids, out,
    st_in, xn, gath, att_out, att_in, st_out, wm_all, wm_t, counts,
    x_send, x_recv, a_send, a_recv, s_send, s_recv, m_send, m_recv,
):
    virtual, tokens, width = stream.shape
    local_heads, hs = wq.shape[1], wq.shape[2]
    heads = width // hs
    seq = tokens * peers
    blocks = seq // BLK
    randoms = ids.shape[2]
    s = lax.axis_index("segment")
    f = lax.axis_index("fsdp")
    ahead = lax.rem(s + 1, segments)
    behind = lax.rem(s + segments - 1, segments)

    barrier = pltpu.get_barrier_semaphore()
    for d in range(1, peers):
        pl.semaphore_signal(barrier, inc=1, device_id=(s, lax.rem(f + d, peers)), device_id_type=MESH)
    for other in (ahead, behind):
        pl.semaphore_signal(barrier, inc=1, device_id=(other, f), device_id_type=MESH)
    pl.semaphore_wait(barrier, peers + 1)

    def to_peer(d):
        return lax.rem(f + d, peers)

    def from_peer(d):
        return lax.rem(f + peers - d, peers)

    def x_copy(r, v, d, landing=False):
        slot = from_peer(d) if landing else f
        return pltpu.make_async_remote_copy(
            src_ref=xn.at[r, v, to_peer(d)], dst_ref=gath.at[r, v, slot],
            send_sem=x_send.at[r, v, d - 1], recv_sem=x_recv.at[r, v, d - 1],
            device_id=(s, to_peer(d)), device_id_type=MESH)

    def a_copy(r, v, d, landing=False):
        slot = from_peer(d) if landing else f
        return pltpu.make_async_remote_copy(
            src_ref=att_out.at[r, v, to_peer(d)], dst_ref=att_in.at[r, v, slot],
            send_sem=a_send.at[r, v, d - 1], recv_sem=a_recv.at[r, v, d - 1],
            device_id=(s, to_peer(d)), device_id_type=MESH)

    def m_copy(d, landing=False):
        slot = from_peer(d) if landing else f
        return pltpu.make_async_remote_copy(
            src_ref=wm, dst_ref=wm_all.at[slot],
            send_sem=m_send.at[d - 1], recv_sem=m_recv.at[d - 1],
            device_id=(s, to_peer(d)), device_id_type=MESH)

    def s_copy(r, v, landing=False):
        at = v if landing else lax.rem(v + jnp.where(s == segments - 1, 1, 0), virtual)
        target = out if r == ROUNDS - 1 else st_in.at[r]
        return pltpu.make_async_remote_copy(
            src_ref=st_out.at[r, v], dst_ref=target.at[at],
            send_sem=s_send.at[r, v], recv_sem=s_recv.at[r, at],
            device_id=(ahead, f), device_id_type=MESH)

    def state_of(r):
        return stream if r == 0 else st_in.at[r - 1]

    def order(r):
        return [lax.rem(o + jnp.where(s < r, 1, 0), virtual) for o in range(virtual)]

    def norm(r, v):
        state = state_of(r)

        def rows_body(i, carry):
            rows = pl.ds(pl.multiple_of(i * 16, 16), 16)
            total = jnp.zeros((16, LANES), F32)
            for c in range(width // LANES):
                wide = state[v, rows, c * LANES:(c + 1) * LANES].astype(F32)
                total = total + wide * wide
            scale = lax.rsqrt(jnp.sum(total, axis=1, keepdims=True) / width + EPS)
            for c in range(heads):
                wide = state[v, rows, c * hs:(c + 1) * hs].astype(F32)
                g = gain[v, :, c * hs:(c + 1) * hs].astype(F32)
                j, at = c // local_heads, (c % local_heads) * hs
                xn[r, v, j, rows, at:at + hs] = (wide * scale * g).astype(BF16)
            return carry

        lax.fori_loop(0, tokens // 16, rows_body, 0)

    def count_blocks():
        lane_block = lax.broadcasted_iota(jnp.int32, (BLK, seq), 1) // BLK
        for v in range(virtual):
            for i in range(blocks):
                window = [(i - 1) % blocks, i, (i + 1) % blocks, 0]
                total = jnp.zeros((BLK, seq), F32)
                for b in window:
                    total = total + jnp.where(lane_block == b, 1.0, 0.0)
                for k in range(randoms):
                    total = total + jnp.where(lane_block == ids[v, i, k], 1.0, 0.0)
                counts[v, i * BLK:(i + 1) * BLK, :] = total

    def attention(r, v):
        step = 4 if local_heads % 4 == 0 else 1

        def one_head(h):
            lanes = pl.ds(pl.multiple_of(h * hs, hs), hs)
            x = gath[r, v, :, :, lanes].reshape(seq, hs)
            q = (jnp.dot(x, wq[v, h], preferred_element_type=F32) * hs ** (-0.5)).astype(BF16)
            k = jnp.dot(x, wk[v, h], preferred_element_type=F32).astype(BF16)
            val = jnp.dot(x, wv[v, h], preferred_element_type=F32).astype(BF16)
            scores = lax.dot_general(q, k, (((1,), (1,)), ((), ())), preferred_element_type=F32)
            count = counts[v]
            scores = jnp.where(count > 0.0, scores, -3e38)
            powers = jnp.exp(scores - jnp.max(scores, axis=1, keepdims=True)) * count
            weights = (powers * (1.0 / jnp.sum(powers, axis=1, keepdims=True))).astype(BF16)
            att = jnp.dot(weights, val, preferred_element_type=F32).astype(BF16)
            att_out[r, v, :, :, lanes] = att.reshape(peers, tokens, hs)

        def body(i, carry):
            for u in range(step):
                one_head(i * step + u)
            return carry

        lax.fori_loop(0, local_heads // step, body, 0)

    def turn_mix():
        wm_all[f] = wm[...]
        for v in range(virtual):
            def body(i, carry):
                at = pl.ds(pl.multiple_of(i * LANES, LANES), LANES)
                part = wm_all[:, v, :, at].reshape(hs, LANES).astype(F32)
                wm_t[v, at, :] = part.T
                return carry
            lax.fori_loop(0, heads * heads // LANES, body, 0)

    def mix(r, v):
        state = state_of(r)
        half = 32
        on = jnp.full((half, hs), live[v].astype(F32))

        def body(i, carry):
            group = i // (tokens // half)
            rows = pl.ds(pl.multiple_of(lax.rem(i, tokens // half) * half, half), half)
            sums = [jnp.zeros((half, hs), F32) for _ in range(8)]
            for h in range(heads):
                j, at = h // local_heads, (h % local_heads) * hs
                a = att_in[r, v, j, rows, at:at + hs].astype(F32)
                w = wm_t[v, pl.ds(pl.multiple_of(h * heads + group * 8, 8), 8), :]
                for g in range(8):
                    sums[g] = sums[g] + a * w[g:g + 1]
            for g in range(8):
                lanes = pl.ds(pl.multiple_of((group * 8 + g) * hs, hs), hs)
                wide = state[v, rows, lanes].astype(F32)
                updated = wide + sums[g].astype(BF16).astype(F32)
                st_out[r, v, rows, lanes] = jnp.where(on > 0.0, updated, wide).astype(BF16)
            return carry

        lax.fori_loop(0, (heads // 8) * (tokens // half), body, 0)

    for r in range(ROUNDS):
        todo = order(r)
        for v in todo:
            if r > 0:
                s_copy(r - 1, v, landing=True).wait_recv()
            norm(r, v)
            for d in range(1, peers):
                x_copy(r, v, d).start()
            gath[r, v, f] = xn[r, v, f]
        if r == 0:
            for d in range(1, peers):
                m_copy(d).start()
            count_blocks()
        for v in todo:
            for d in range(1, peers):
                x_copy(r, v, d, landing=True).wait_recv()
            attention(r, v)
            for d in range(1, peers):
                a_copy(r, v, d).start()
            att_in[r, v, f] = att_out[r, v, f]
        if r == 0:
            for d in range(1, peers):
                m_copy(d, landing=True).wait_recv()
            turn_mix()
        for v in todo:
            for d in range(1, peers):
                a_copy(r, v, d, landing=True).wait_recv()
            mix(r, v)
            s_copy(r, v).start()

    for v in range(virtual):
        s_copy(ROUNDS - 1, v, landing=True).wait_recv()
    for r in range(ROUNDS):
        for v in range(virtual):
            for d in range(1, peers):
                x_copy(r, v, d).wait_send()
                a_copy(r, v, d).wait_send()
            s_copy(r, v).wait_send()
    for d in range(1, peers):
        m_copy(d).wait_send()


def shards(segments, peers, stream, gain, w_query, w_key, w_value, w_mix, active, random_blocks):
    virtual, _, tokens, width = stream.shape
    local_heads, hs = w_query.shape[2], w_query.shape[3]
    heads = width // hs
    local = w_mix.shape[2]
    seq = tokens * peers
    group = local_heads * hs
    vmem = pl.BlockSpec(memory_space=pltpu.VMEM)
    smem = pl.BlockSpec(memory_space=pltpu.SMEM)
    dma = pltpu.SemaphoreType.DMA
    apart = max(peers - 1, 1)
    result = pl.pallas_call(
        functools.partial(kernel, segments, peers),
        out_shape=jax.ShapeDtypeStruct((virtual, tokens, width), BF16),
        in_specs=[vmem] * 6 + [smem] * 2,
        out_specs=pl.BlockSpec(memory_space=pl.ANY),
        scratch_shapes=[
            pltpu.VMEM((max(ROUNDS - 1, 1), virtual, tokens, width), BF16),
            pltpu.VMEM((ROUNDS, virtual, peers, tokens, group), BF16),
            pltpu.VMEM((ROUNDS, virtual, peers, tokens, group), BF16),
            pltpu.VMEM((ROUNDS, virtual, peers, tokens, group), BF16),
            pltpu.VMEM((ROUNDS, virtual, peers, tokens, group), BF16),
            pltpu.VMEM((ROUNDS, virtual, tokens, width), BF16),
            pltpu.VMEM((peers, virtual, local, heads * heads), BF16),
            pltpu.VMEM((virtual, heads * heads, hs), F32),
            pltpu.VMEM((virtual, seq, seq), F32),
            dma((ROUNDS, virtual, apart)),
            dma((ROUNDS, virtual, apart)),
            dma((ROUNDS, virtual, apart)),
            dma((ROUNDS, virtual, apart)),
            dma((ROUNDS, virtual)),
            dma((ROUNDS, virtual)),
            dma((apart,)),
            dma((apart,)),
        ],
        compiler_params=pltpu.CompilerParams(
            collective_id=0, has_side_effects=True, vmem_limit_bytes=56 * 1024 * 1024
        ),
        cost_estimate=pl.CostEstimate(
            flops=ROUNDS * virtual * seq * local_heads * hs * (6 * hs + 4 * seq),
            bytes_accessed=6 * 1024 * 1024,
            transcendentals=ROUNDS * virtual * seq * local_heads * seq,
        ),
    )(
        stream[:, 0],
        gain.reshape(virtual, 1, width),
        w_query[:, 0],
        w_key[:, 0],
        w_value[:, 0],
        w_mix.reshape(virtual, local, heads * heads),
        active[:, 0],
        random_blocks[:, 0],
    )
    return result[:, None]


def solution(mesh):
    in_specs = (
        P(None, "segment", "fsdp", None),
        P(None, "segment", None),
        P(None, "segment", "fsdp", None, None),
        P(None, "segment", "fsdp", None, None),
        P(None, "segment", "fsdp", None, None),
        P(None, "segment", "fsdp", None, None),
        P(None, "segment"),
        P(None, "segment", None, None),
    )
    out_specs = P(None, "segment", "fsdp", None)
    body = functools.partial(shards, mesh.shape["segment"], mesh.shape["fsdp"])
    return jax.shard_map(body, mesh=mesh, in_specs=in_specs, out_specs=out_specs, check_vma=False)
```

time: 286 us -> 83.5 us (0.29)
  local copies, waits for them, and re-layouts: 91.9 us -> 5.56 us
  Pallas kernels: 0 us -> 77.7 us
  matrix products: 60.7 us -> 0 us
  waiting for transfers between devices: 58.7 us -> 0 us
  blocking collectives: 45.2 us -> 0 us
  other arithmetic: 15 us -> 0 us
  starting transfers between devices: 12.1 us -> 0 us
    pallas_call x0 -> x1, Pallas kernels: none -> 77.7 us  [shards(): pl.pallas_call(functools.partial(kernel, segments, peers), out_shape=jax....]
    dot_general x22 -> x0, matrix products: 60.7 us -> none  [the longest x4 29.3 us: block_attention(): jnp.einsum('hnqk,hnkd->hnqd', weights, picked_values, preferred_element_t...]
    gather x16 -> x0, local copies, waits for them, and re-layouts: 44.8 us -> none  [the longest x8 22.4 us: block_attention(): value_blocks[:, chosen]]
    ppermute x2 -> x0, waiting for transfers between devices: 34 us -> none  [shifted(): lax.ppermute(value, axis, [(i, (i + by) % devices) for i in range(devices)])]
    all_gather x1 -> x0, blocking collectives: 31.9 us -> none  [mix_heads(): lax.all_gather(mix_w, 'fsdp', axis=1, tiled=True)]
    all_to_all x3 -> x0, waiting for transfers between devices: 24.7 us -> none  [the longest x2 24.7 us: token_layer(): lax.all_to_all(view, 'fsdp', split_axis=2, concat_axis=1, tiled=True)]
    convert_element_type x5 -> x0, local copies, waits for them, and re-layouts: 14.5 us -> none  [the longest x4 13.2 us: token_layer(): mixed.reshape(wide.shape).astype(jnp.float32)]
    all_to_all x1 -> x0, blocking collectives: 13.2 us -> none  [token_layer(): lax.all_to_all(attended, 'fsdp', split_axis=2, concat_axis=1, tiled=True)]
  transfers between devices with their start and end apart: 5 -> 0, of which waited for: 4 -> 0; matrix products, arithmetic and copies ran while one was open for 1% -> 0% of each run, Pallas kernels for 0% -> 0%
where the time goes in v1:
time: 83.5 us; the launch traced here: 83.3 us
  Pallas kernels  77.7 us (93%)
  local copies, waits for them, and re-layouts  5.56 us (7%)
    pallas_call x1, Pallas kernels, shards(): pl.pallas_call(functools.partial(kernel, segments, peers), out_shape=jax....  77.7 us
    unnamed x2, local copies, waits for them, and re-layouts  3.63 us
    reshape x1, local copies, waits for them, and re-layouts, shards(): w_mix.reshape(virtual, local, heads * heads)  1.93 us

profile of v1, /device:TPU:0, one launch (start us, length us, event | category | flops | bytes accessed | tf_op | source)
XLA Modules:
  0.0 83.3 jit_solution(4904141762631702524)
XLA Ops:
  0.0 1.3 %copy.12.gain = bf16[2,1,4096]{2,1,0:T(2,128)(2,1)} copy(bf16[2,1,4096]{2,0,1:T(2,128)(2,1)} %param.9) | data formatting | bytes 32768 | tf_op args[1]
  1.3 1.9 %copy.13.wm = bf16[2,64,1024]{2,1,0:T(8,128)(2,1)} copy(bf16[2,64,1024]{1,2,0:T(8,128)(2,1)} %bitcast.15) | data formatting | bytes 524288 | tf_op jit(solution)/shard_map/reshape | solution.py:263
  3.3 77.7 %shard_map.82 = bf16[2,64,4096]{2,1,0:T(8,128)(2,1)} custom-call(bf16[2,64,4096]{2,1,0:T(8,128)(2,1)} %bitcast.11, bf16[2,1,4096]{2,1,0:T(2,128)(2,1)} %copy.12.gain, bf16[2,16,128,128]{3,2,1,0:T(8,128)(2,1)} %bitcast.12, bf16[2,16,128,128]{3,2,1,0:T(8,128)(2,1)} %bitcast.13, bf16[2,16,128,128]{3,2,1,0:T(8,128)(2,1)} %bitcast.14, ...), custom_call_target="tpu_custom_call" | custom-call | flops 1342177280 | bytes 6291456 | tf_op jit(solution)/shard_map/pallas_call | solution.py:225
  81.0 2.3 %copy.16 = bf16[2,1,64,4096]{3,2,1,0:T(8,128)(2,1)} copy(bf16[2,1,64,4096]{3,2,1,0:T(8,128)(2,1)} %bitcast.10) | data formatting | bytes 2097152

commit v2 on v1

v2 whole, which is shorter than its diff:
```python
import functools

import jax
import jax.numpy as jnp
from jax import lax
from jax.experimental import pallas as pl
from jax.experimental.pallas import tpu as pltpu
from jax.sharding import PartitionSpec as P

BLK = 64
ROUNDS = 2
EPS = 1e-05
LANES = 128
PIECES = 2
MESH = pl.DeviceIdType.MESH
F32 = jnp.float32
BF16 = jnp.bfloat16


def kernel(
    segments, peers, stream_hbm, gain_in, wq_hbm, wk_hbm, wv_hbm, wm, live, ids, out,
    stream, gain, wq, wk, wv,
    st_in, xn, gath, att_out, att_in, st_out, wm_all, wm_t, counts,
    x_send, x_recv, a_send, a_recv, s_send, s_recv, m_send, m_recv, load_sem,
):
    virtual, tokens, width = stream.shape
    local_heads, hs = wq.shape[1], wq.shape[2]
    half = tokens // PIECES
    part = local_heads // PIECES
    local = wm.shape[2]
    heads = width // hs
    seq = tokens * peers
    blocks = seq // BLK
    randoms = ids.shape[2]
    s = lax.axis_index("segment")
    f = lax.axis_index("fsdp")
    ahead = lax.rem(s + 1, segments)
    behind = lax.rem(s + segments - 1, segments)

    barrier = pltpu.get_barrier_semaphore()
    for d in range(1, peers):
        pl.semaphore_signal(barrier, inc=1, device_id=(s, lax.rem(f + d, peers)), device_id_type=MESH)
    for other in (ahead, behind):
        pl.semaphore_signal(barrier, inc=1, device_id=(other, f), device_id_type=MESH)

    def load(n, v):
        source, target = ((stream_hbm, stream), (wq_hbm, wq), (wk_hbm, wk), (wv_hbm, wv))[n]
        return pltpu.make_async_copy(source.at[v], target.at[v], load_sem.at[n, v])

    for n in range(4):
        for v in range(virtual):
            load(n, v).start()

    def to_peer(d):
        return lax.rem(f + d, peers)

    def from_peer(d):
        return lax.rem(f + peers - d, peers)

    def x_copy(r, v, d, pc, hh, landing=False):
        slot = from_peer(d) if landing else f
        rows, lanes = pl.ds(pc * half, half), pl.ds(hh * part * hs, part * hs)
        return pltpu.make_async_remote_copy(
            src_ref=xn.at[r, v, to_peer(d), rows, lanes], dst_ref=gath.at[r, v, slot, rows, lanes],
            send_sem=x_send.at[r, v, d - 1, pc, hh], recv_sem=x_recv.at[r, v, d - 1, pc, hh],
            device_id=(s, to_peer(d)), device_id_type=MESH)

    def a_copy(r, v, d, pc, hh, landing=False):
        slot = from_peer(d) if landing else f
        rows, lanes = pl.ds(pc * half, half), pl.ds(hh * part * hs, part * hs)
        return pltpu.make_async_remote_copy(
            src_ref=att_out.at[r, v, to_peer(d), rows, lanes], dst_ref=att_in.at[r, v, slot, rows, lanes],
            send_sem=a_send.at[r, v, d - 1, pc, hh], recv_sem=a_recv.at[r, v, d - 1, pc, hh],
            device_id=(s, to_peer(d)), device_id_type=MESH)

    def m_copy(d, landing=False):
        slot = from_peer(d) if landing else f
        return pltpu.make_async_remote_copy(
            src_ref=wm_all.at[f], dst_ref=wm_all.at[slot],
            send_sem=m_send.at[d - 1], recv_sem=m_recv.at[d - 1],
            device_id=(s, to_peer(d)), device_id_type=MESH)

    def s_copy(r, v, pc, landing=False):
        at = v if landing else lax.rem(v + jnp.where(s == segments - 1, 1, 0), virtual)
        target = out if r == ROUNDS - 1 else st_in.at[r]
        rows = pl.ds(pc * half, half)
        return pltpu.make_async_remote_copy(
            src_ref=st_out.at[r, v, rows], dst_ref=target.at[at, rows],
            send_sem=s_send.at[r, v, pc], recv_sem=s_recv.at[r, at, pc],
            device_id=(ahead, f), device_id_type=MESH)

    def state_of(r):
        return stream if r == 0 else st_in.at[r - 1]

    def order(r):
        if r == 0:
            return list(range(virtual))
        return [lax.rem(o + jnp.where(s < r, 1, 0), virtual) for o in range(virtual)]

    def norm(r, v, pc):
        state = state_of(r)

        def rows_body(i, carry):
            rows = pl.ds(pl.multiple_of(pc * half + i * 16, 16), 16)
            total = jnp.zeros((16, LANES), F32)
            for c in range(width // LANES):
                wide = state[v, rows, c * LANES:(c + 1) * LANES].astype(F32)
                total = total + wide * wide
            scale = lax.rsqrt(jnp.sum(total, axis=1, keepdims=True) / width + EPS)
            for c in range(heads):
                wide = state[v, rows, c * hs:(c + 1) * hs].astype(F32)
                g = gain[v, :, c * hs:(c + 1) * hs]
                j, at = c // local_heads, (c % local_heads) * hs
                xn[r, v, j, rows, at:at + hs] = (wide * scale * g).astype(BF16)
            return carry

        lax.fori_loop(0, half // 16, rows_body, 0)

    def count_blocks():
        lane_block = lax.broadcasted_iota(jnp.int32, (BLK, seq), 1) // BLK
        for v in range(virtual):
            for i in range(blocks):
                window = [(i - 1) % blocks, i, (i + 1) % blocks, 0]
                total = jnp.zeros((BLK, seq), F32)
                for b in window:
                    total = total + jnp.where(lane_block == b, 1.0, 0.0)
                for k in range(randoms):
                    total = total + jnp.where(lane_block == ids[v, i, k], 1.0, 0.0)
                counts[v, i * BLK:(i + 1) * BLK, :] = total

    def attention(r, v, hh):
        step = 4 if part % 4 == 0 else 1

        def one_head(h):
            lanes = pl.ds(pl.multiple_of(h * hs, hs), hs)
            x = gath[r, v, :, :, lanes].reshape(seq, hs)
            q = (jnp.dot(x, wq[v, h], preferred_element_type=F32) * hs ** (-0.5)).astype(BF16)
            k = jnp.dot(x, wk[v, h], preferred_element_type=F32).astype(BF16)
            val = jnp.dot(x, wv[v, h], preferred_element_type=F32).astype(BF16)
            scores = lax.dot_general(q, k, (((1,), (1,)), ((), ())), preferred_element_type=F32)
            count = counts[v]
            scores = jnp.where(count > 0.0, scores, -3e38)
            powers = jnp.exp(scores - jnp.max(scores, axis=1, keepdims=True)) * count
            weights = (powers * (1.0 / jnp.sum(powers, axis=1, keepdims=True))).astype(BF16)
            att = jnp.dot(weights, val, preferred_element_type=F32).astype(BF16)
            att_out[r, v, :, :, lanes] = att.reshape(peers, tokens, hs)

        def body(i, carry):
            for u in range(step):
                one_head(hh * part + i * step + u)
            return carry

        lax.fori_loop(0, part // step, body, 0)

    def pack_mix():
        def body(i, carry):
            rows = pl.ds(pl.multiple_of(i * LANES, LANES), LANES)
            both = [wm[v, rows, :].astype(F32) for v in range(virtual)]
            wm_all[f, rows, :] = jnp.concatenate(both, axis=1).astype(BF16)
            return carry

        lax.fori_loop(0, heads * heads // LANES, body, 0)

    def spread_mix():
        def body(i, carry):
            rows = pl.ds(pl.multiple_of(i * LANES, LANES), LANES)
            each = [wm_all[j, rows, :].astype(F32) for j in range(peers)]
            for v in range(virtual):
                wm_t[v, rows, :] = jnp.concatenate(
                    [e[:, v * local:(v + 1) * local] for e in each], axis=1)
            return carry

        lax.fori_loop(0, heads * heads // LANES, body, 0)

    def mix(r, v, pc):
        state = state_of(r)
        on = jnp.full((half, hs), live[v].astype(F32))

        rows = pl.ds(pc * half, half)

        def body(group, carry):
            sums = [jnp.zeros((half, hs), F32) for _ in range(8)]
            for h in range(heads):
                j, at = h // local_heads, (h % local_heads) * hs
                a = att_in[r, v, j, rows, at:at + hs].astype(F32)
                w = wm_t[v, pl.ds(pl.multiple_of(h * heads + group * 8, 8), 8), :]
                for g in range(8):
                    sums[g] = sums[g] + a * w[g:g + 1]
            for g in range(8):
                lanes = pl.ds(pl.multiple_of((group * 8 + g) * hs, hs), hs)
                wide = state[v, rows, lanes].astype(F32)
                updated = wide + sums[g].astype(BF16).astype(F32)
                st_out[r, v, rows, lanes] = jnp.where(on > 0.0, updated, wide).astype(BF16)
            return carry

        lax.fori_loop(0, heads // 8, body, 0)

    others = range(1, peers)
    pieces = range(PIECES)
    for r in range(ROUNDS):
        todo = order(r)
        for o, v in enumerate(todo):
            if r == 0:
                load(0, v).wait()
                gain[v] = gain_in[v:v + 1, :].astype(F32)
            for pc in pieces:
                if r > 0:
                    s_copy(r - 1, v, pc, landing=True).wait_recv()
                norm(r, v, pc)
                if r == 0 and o == 0 and pc == 0:
                    pl.semaphore_wait(barrier, peers + 1)
                for hh in pieces:
                    for d in others:
                        x_copy(r, v, d, pc, hh).start()
            gath[r, v, f] = xn[r, v, f]
        if r == 0:
            pack_mix()
            for d in others:
                m_copy(d).start()
            count_blocks()
        for v in todo:
            if r == 0:
                for n in range(1, 4):
                    load(n, v).wait()
            for hh in pieces:
                for d in others:
                    for pc in pieces:
                        x_copy(r, v, d, pc, hh, landing=True).wait_recv()
                attention(r, v, hh)
                for pc in pieces:
                    for d in others:
                        a_copy(r, v, d, pc, hh).start()
            att_in[r, v, f] = att_out[r, v, f]
        if r == 0:
            for d in others:
                m_copy(d, landing=True).wait_recv()
            spread_mix()
        for v in todo:
            for pc in pieces:
                for d in others:
                    for hh in pieces:
                        a_copy(r, v, d, pc, hh, landing=True).wait_recv()
                mix(r, v, pc)
                s_copy(r, v, pc).start()

    for v in range(virtual):
        for pc in pieces:
            s_copy(ROUNDS - 1, v, pc, landing=True).wait_recv()
    for r in range(ROUNDS):
        for v in range(virtual):
            for pc in pieces:
                for d in others:
                    for hh in pieces:
                        x_copy(r, v, d, pc, hh).wait_send()
                        a_copy(r, v, d, pc, hh).wait_send()
                s_copy(r, v, pc).wait_send()
    for d in others:
        m_copy(d).wait_send()


def shards(segments, peers, stream, gain, w_query, w_key, w_value, w_mix, active, random_blocks):
    virtual, _, tokens, width = stream.shape
    local_heads, hs = w_query.shape[2], w_query.shape[3]
    heads = width // hs
    local = w_mix.shape[2]
    seq = tokens * peers
    group = local_heads * hs
    vmem = pl.BlockSpec(memory_space=pltpu.VMEM)
    hbm = pl.BlockSpec(memory_space=pl.ANY)
    smem = pl.BlockSpec(memory_space=pltpu.SMEM)
    dma = pltpu.SemaphoreType.DMA
    apart = max(peers - 1, 1)
    result = pl.pallas_call(
        functools.partial(kernel, segments, peers),
        out_shape=jax.ShapeDtypeStruct((virtual, tokens, width), BF16),
        in_specs=[hbm, vmem, hbm, hbm, hbm, vmem, smem, smem],
        out_specs=pl.BlockSpec(memory_space=pl.ANY),
        scratch_shapes=[
            pltpu.VMEM((virtual, tokens, width), BF16),
            pltpu.VMEM((virtual, 1, width), F32),
            pltpu.VMEM((virtual, local_heads, hs, hs), BF16),
            pltpu.VMEM((virtual, local_heads, hs, hs), BF16),
            pltpu.VMEM((virtual, local_heads, hs, hs), BF16),
            pltpu.VMEM((max(ROUNDS - 1, 1), virtual, tokens, width), BF16),
            pltpu.VMEM((ROUNDS, virtual, peers, tokens, group), BF16),
            pltpu.VMEM((ROUNDS, virtual, peers, tokens, group), BF16),
            pltpu.VMEM((ROUNDS, virtual, peers, tokens, group), BF16),
            pltpu.VMEM((ROUNDS, virtual, peers, tokens, group), BF16),
            pltpu.VMEM((ROUNDS, virtual, tokens, width), BF16),
            pltpu.VMEM((peers, heads * heads, virtual * local), BF16),
            pltpu.VMEM((virtual, heads * heads, hs), F32),
            pltpu.VMEM((virtual, seq, seq), F32),
            dma((ROUNDS, virtual, apart, PIECES, PIECES)),
            dma((ROUNDS, virtual, apart, PIECES, PIECES)),
            dma((ROUNDS, virtual, apart, PIECES, PIECES)),
            dma((ROUNDS, virtual, apart, PIECES, PIECES)),
            dma((ROUNDS, virtual, PIECES)),
            dma((ROUNDS, virtual, PIECES)),
            dma((apart,)),
            dma((apart,)),
            dma((4, virtual)),
        ],
        compiler_params=pltpu.CompilerParams(
            collective_id=0, has_side_effects=True, vmem_limit_bytes=56 * 1024 * 1024
        ),
        cost_estimate=pl.CostEstimate(
            flops=ROUNDS * virtual * seq * local_heads * hs * (6 * hs + 4 * seq),
            bytes_accessed=6 * 1024 * 1024,
            transcendentals=ROUNDS * virtual * seq * local_heads * seq,
        ),
    )(
        stream[:, 0],
        gain[:, 0],
        w_query[:, 0],
        w_key[:, 0],
        w_value[:, 0],
        w_mix[:, 0].transpose(0, 2, 3, 1).reshape(virtual, heads * heads, local),
        active[:, 0],
        random_blocks[:, 0],
    )
    return result[:, None]


def solution(mesh):
    in_specs = (
        P(None, "segment", "fsdp", None),
        P(None, "segment", None),
        P(None, "segment", "fsdp", None, None),
        P(None, "segment", "fsdp", None, None),
        P(None, "segment", "fsdp", None, None),
        P(None, "segment", "fsdp", None, None),
        P(None, "segment"),
        P(None, "segment", None, None),
    )
    out_specs = P(None, "segment", "fsdp", None)
    body = functools.partial(shards, mesh.shape["segment"], mesh.shape["fsdp"])
    return jax.shard_map(body, mesh=mesh, in_specs=in_specs, out_specs=out_specs, check_vma=False)
```

time: 83.5 us -> 75 us (0.90)
  Pallas kernels: 77.7 us -> 72.5 us
  local copies, waits for them, and re-layouts: 5.56 us -> 2.29 us
    pallas_call x1, Pallas kernels: 77.7 us -> 72.5 us  [shards(): pl.pallas_call(functools.partial(kernel, segments, peers), out_shape=jax....]
    reshape x1 -> x0, local copies, waits for them, and re-layouts: 1.93 us -> none  [shards(): w_mix.reshape(virtual, local, heads * heads)]
    unnamed x2 -> x1, local copies, waits for them, and re-layouts: 3.63 us -> 2.29 us
where the time goes in v2:
time: 75 us; the launch traced here: 74.8 us
  Pallas kernels  72.5 us (97%)
  local copies, waits for them, and re-layouts  2.29 us (3%)
    pallas_call x1, Pallas kernels, shards(): pl.pallas_call(functools.partial(kernel, segments, peers), out_shape=jax....  72.5 us
    unnamed x1, local copies, waits for them, and re-layouts  2.29 us

profile of v2, /device:TPU:0, one launch (start us, length us, event | category | flops | bytes accessed | tf_op | source)
XLA Modules:
  0.0 74.8 jit_solution(11654579808494778532)
XLA Ops:
  0.0 72.5 %shard_map.82 = bf16[2,64,4096]{2,1,0:T(8,128)(2,1)} custom-call(bf16[2,64,4096]{2,1,0:T(8,128)(2,1)} %bitcast.16, bf16[2,4096]{1,0:T(2,128)(2,1)} %bitcast.21, bf16[2,16,128,128]{3,2,1,0:T(8,128)(2,1)} %bitcast.17, bf16[2,16,128,128]{3,2,1,0:T(8,128)(2,1)} %bitcast.18, bf16[2,16,128,128]{3,2,1,0:T(8,128)(2,1)} %bitcast.19, bf16[2,1024,64]{2,1,0:T(8,128)(2,1)} %bitcast.20, ...), custom_call_target="tpu_custom_call" | custom-call | flops 1342177280 | bytes 6291456 | tf_op jit(solution)/shard_map/pallas_call | solution.py:273
  72.5 2.3 %copy.11 = bf16[2,1,64,4096]{3,2,1,0:T(8,128)(2,1)} copy(bf16[2,1,64,4096]{3,2,1,0:T(8,128)(2,1)} %bitcast.15) | data formatting | bytes 2097152

commit v3 on v2

--- a/solution.py
+++ b/solution.py
@@ -197,6 +197,26 @@
 
     others = range(1, peers)
     pieces = range(PIECES)
+    def send_x(r, v, pc):
+        for hh in pieces:
+            for d in others:
+                x_copy(r, v, d, pc, hh).start()
+
+    def send_a(r, v, hh):
+        for pc in pieces:
+            for d in others:
+                a_copy(r, v, d, pc, hh).start()
+
+    def wait_x(r, v, hh):
+        for d in others:
+            for pc in pieces:
+                x_copy(r, v, d, pc, hh, landing=True).wait_recv()
+
+    def wait_a(r, v, pc):
+        for d in others:
+            for hh in pieces:
+                a_copy(r, v, d, pc, hh, landing=True).wait_recv()
+
     for r in range(ROUNDS):
         todo = order(r)
         for o, v in enumerate(todo):
@@ -209,37 +229,39 @@
                 norm(r, v, pc)
                 if r == 0 and o == 0 and pc == 0:
                     pl.semaphore_wait(barrier, peers + 1)
-                for hh in pieces:
-                    for d in others:
-                        x_copy(r, v, d, pc, hh).start()
+                if o == 0:
+                    send_x(r, v, pc)
             gath[r, v, f] = xn[r, v, f]
         if r == 0:
             pack_mix()
-            for d in others:
-                m_copy(d).start()
             count_blocks()
-        for v in todo:
+        for o, v in enumerate(todo):
             if r == 0:
                 for n in range(1, 4):
                     load(n, v).wait()
             for hh in pieces:
-                for d in others:
-                    for pc in pieces:
-                        x_copy(r, v, d, pc, hh, landing=True).wait_recv()
+                wait_x(r, v, hh)
+                if hh == 0:
+                    if o + 1 < virtual:
+                        for pc in pieces:
+                            send_x(r, todo[o + 1], pc)
+                    if r == 0 and o == 0:
+                        for d in others:
+                            m_copy(d).start()
                 attention(r, v, hh)
-                for pc in pieces:
-                    for d in others:
-                        a_copy(r, v, d, pc, hh).start()
+                if o == 0:
+                    send_a(r, v, hh)
             att_in[r, v, f] = att_out[r, v, f]
         if r == 0:
             for d in others:
                 m_copy(d, landing=True).wait_recv()
             spread_mix()
-        for v in todo:
+        for o, v in enumerate(todo):
             for pc in pieces:
-                for d in others:
+                wait_a(r, v, pc)
+                if pc == 0 and o + 1 < virtual:
                     for hh in pieces:
-                        a_copy(r, v, d, pc, hh, landing=True).wait_recv()
+                        send_a(r, todo[o + 1], hh)
                 mix(r, v, pc)
                 s_copy(r, v, pc).start()
 

time: 75 us -> 74.6 us (level)
  no operation moved by 1% of the time
where the time goes in v3:
time: 74.6 us; the launch traced here: 74.4 us
  Pallas kernels  72.1 us (97%)
  local copies, waits for them, and re-layouts  2.29 us (3%)
    pallas_call x1, Pallas kernels, shards(): pl.pallas_call(functools.partial(kernel, segments, peers), out_shape=jax....  72.1 us
    unnamed x1, local copies, waits for them, and re-layouts  2.29 us

profile of v3, /device:TPU:0, one launch (start us, length us, event | category | flops | bytes accessed | tf_op | source)
XLA Modules:
  0.0 74.4 jit_solution(2318678163126100348)
XLA Ops:
  0.0 72.1 %shard_map.82 = bf16[2,64,4096]{2,1,0:T(8,128)(2,1)} custom-call(bf16[2,64,4096]{2,1,0:T(8,128)(2,1)} %bitcast.16, bf16[2,4096]{1,0:T(2,128)(2,1)} %bitcast.21, bf16[2,16,128,128]{3,2,1,0:T(8,128)(2,1)} %bitcast.17, bf16[2,16,128,128]{3,2,1,0:T(8,128)(2,1)} %bitcast.18, bf16[2,16,128,128]{3,2,1,0:T(8,128)(2,1)} %bitcast.19, bf16[2,1024,64]{2,1,0:T(8,128)(2,1)} %bitcast.20, ...), custom_call_target="tpu_custom_call" | custom-call | flops 1342177280 | bytes 6291456 | tf_op jit(solution)/shard_map/pallas_call | solution.py:295
  72.1 2.3 %copy.11 = bf16[2,1,64,4096]{3,2,1,0:T(8,128)(2,1)} copy(bf16[2,1,64,4096]{3,2,1,0:T(8,128)(2,1)} %bitcast.15) | data formatting | bytes 2097152

commit v4 on v3

--- a/solution.py
+++ b/solution.py
@@ -131,23 +131,38 @@
     def attention(r, v, hh):
         step = 4 if part % 4 == 0 else 1
 
-        def one_head(h):
-            lanes = pl.ds(pl.multiple_of(h * hs, hs), hs)
-            x = gath[r, v, :, :, lanes].reshape(seq, hs)
-            q = (jnp.dot(x, wq[v, h], preferred_element_type=F32) * hs ** (-0.5)).astype(BF16)
-            k = jnp.dot(x, wk[v, h], preferred_element_type=F32).astype(BF16)
-            val = jnp.dot(x, wv[v, h], preferred_element_type=F32).astype(BF16)
-            scores = lax.dot_general(q, k, (((1,), (1,)), ((), ())), preferred_element_type=F32)
+        ones = jnp.ones((seq, hs), BF16)
+
+        def body(i, carry):
+            mine = [hh * part + i * step + u for u in range(step)]
+            lanes = [pl.ds(pl.multiple_of(h * hs, hs), hs) for h in mine]
+            x = [gath[r, v, :, :, at].reshape(seq, hs) for at in lanes]
+            qk = [
+                jnp.dot(x[u], jnp.concatenate([wq[v, h], wk[v, h]], axis=1), preferred_element_type=F32)
+                for u, h in enumerate(mine)
+            ]
+            q = [(a[:, :hs] * hs ** (-0.5)).astype(BF16) for a in qk]
+            k = [a[:, hs:].astype(BF16) for a in qk]
+            scores = [
+                lax.dot_general(a, b, (((1,), (1,)), ((), ())), preferred_element_type=F32)
+                for a, b in zip(q, k)
+            ]
+            val = [
+                jnp.dot(x[u], wv[v, h], preferred_element_type=F32).astype(BF16)
+                for u, h in enumerate(mine)
+            ]
             count = counts[v]
-            scores = jnp.where(count > 0.0, scores, -3e38)
-            powers = jnp.exp(scores - jnp.max(scores, axis=1, keepdims=True)) * count
-            weights = (powers * (1.0 / jnp.sum(powers, axis=1, keepdims=True))).astype(BF16)
-            att = jnp.dot(weights, val, preferred_element_type=F32).astype(BF16)
-            att_out[r, v, :, :, lanes] = att.reshape(peers, tokens, hs)
-
-        def body(i, carry):
-            for u in range(step):
-                one_head(hh * part + i * step + u)
+            if blocks > 3:
+                scores = [jnp.where(count > 0.0, a, -3e38) for a in scores]
+            top = [jnp.max(a, axis=1, keepdims=True) for a in scores]
+            powers = [(jnp.exp(a - m) * count).astype(BF16) for a, m in zip(scores, top)]
+            sums = [
+                jnp.dot(p, jnp.concatenate([a, ones], axis=1), preferred_element_type=F32)
+                for p, a in zip(powers, val)
+            ]
+            att = [(a[:, :hs] * (1.0 / a[:, hs:])).astype(BF16) for a in sums]
+            for at, a in zip(lanes, att):
+                att_out[r, v, :, :, at] = a.reshape(peers, tokens, hs)
             return carry
 
         lax.fori_loop(0, part // step, body, 0)

time: 74.6 us -> 71.1 us (0.953)
  Pallas kernels: 72.1 us -> 68.6 us
    pallas_call x1, Pallas kernels: 72.1 us -> 68.6 us  [shards(): pl.pallas_call(functools.partial(kernel, segments, peers), out_shape=jax....]
where the time goes in v4:
time: 71.1 us; the launch traced here: 70.9 us
  Pallas kernels  68.6 us (96%)
  local copies, waits for them, and re-layouts  2.29 us (3%)
    pallas_call x1, Pallas kernels, shards(): pl.pallas_call(functools.partial(kernel, segments, peers), out_shape=jax....  68.6 us
    unnamed x1, local copies, waits for them, and re-layouts  2.29 us

profile of v4, /device:TPU:0, one launch (start us, length us, event | category | flops | bytes accessed | tf_op | source)
XLA Modules:
  0.0 70.9 jit_solution(13067223708874867175)
XLA Ops:
  0.0 68.6 %shard_map.82 = bf16[2,64,4096]{2,1,0:T(8,128)(2,1)} custom-call(bf16[2,64,4096]{2,1,0:T(8,128)(2,1)} %bitcast.16, bf16[2,4096]{1,0:T(2,128)(2,1)} %bitcast.21, bf16[2,16,128,128]{3,2,1,0:T(8,128)(2,1)} %bitcast.17, bf16[2,16,128,128]{3,2,1,0:T(8,128)(2,1)} %bitcast.18, bf16[2,16,128,128]{3,2,1,0:T(8,128)(2,1)} %bitcast.19, bf16[2,1024,64]{2,1,0:T(8,128)(2,1)} %bitcast.20, ...), custom_call_target="tpu_custom_call" | custom-call | flops 1342177280 | bytes 6291456 | tf_op jit(solution)/shard_map/pallas_call | solution.py:310
  68.6 2.3 %copy.11 = bf16[2,1,64,4096]{3,2,1,0:T(8,128)(2,1)} copy(bf16[2,1,64,4096]{3,2,1,0:T(8,128)(2,1)} %bitcast.15) | data formatting | bytes 2097152

commit v5 on v4

--- a/solution.py
+++ b/solution.py
@@ -20,8 +20,9 @@
 def kernel(
     segments, peers, stream_hbm, gain_in, wq_hbm, wk_hbm, wv_hbm, wm, live, ids, out,
     stream, gain, wq, wk, wv,
-    st_in, xn, gath, att_out, att_in, st_out, wm_all, wm_t, counts,
+    st_in, xn, gath, att_out, att_in, st_out, wm_all, wm_t, counts, st_ahead, wm_behind, wm_last,
     x_send, x_recv, a_send, a_recv, s_send, s_recv, m_send, m_recv, load_sem,
+    w_send, w_recv, store_sem,
 ):
     virtual, tokens, width = stream.shape
     local_heads, hs = wq.shape[1], wq.shape[2]
@@ -40,8 +41,9 @@
     barrier = pltpu.get_barrier_semaphore()
     for d in range(1, peers):
         pl.semaphore_signal(barrier, inc=1, device_id=(s, lax.rem(f + d, peers)), device_id_type=MESH)
-    for other in (ahead, behind):
-        pl.semaphore_signal(barrier, inc=1, device_id=(other, f), device_id_type=MESH)
+    for d in range(peers):
+        pl.semaphore_signal(barrier, inc=1, device_id=(behind, lax.rem(f + d, peers)), device_id_type=MESH)
+    everyone = 2 * peers - 1
 
     def load(n, v):
         source, target = ((stream_hbm, stream), (wq_hbm, wq), (wk_hbm, wk), (wv_hbm, wv))[n]
@@ -65,13 +67,18 @@
             send_sem=x_send.at[r, v, d - 1, pc, hh], recv_sem=x_recv.at[r, v, d - 1, pc, hh],
             device_id=(s, to_peer(d)), device_id_type=MESH)
 
+    def onward(v):
+        return lax.rem(v + jnp.where(s == segments - 1, 1, 0), virtual)
+
     def a_copy(r, v, d, pc, hh, landing=False):
+        last = r == ROUNDS - 1
         slot = from_peer(d) if landing else f
+        at = onward(v) if last and not landing else v
         rows, lanes = pl.ds(pc * half, half), pl.ds(hh * part * hs, part * hs)
         return pltpu.make_async_remote_copy(
-            src_ref=att_out.at[r, v, to_peer(d), rows, lanes], dst_ref=att_in.at[r, v, slot, rows, lanes],
-            send_sem=a_send.at[r, v, d - 1, pc, hh], recv_sem=a_recv.at[r, v, d - 1, pc, hh],
-            device_id=(s, to_peer(d)), device_id_type=MESH)
+            src_ref=att_out.at[r, v, to_peer(d), rows, lanes], dst_ref=att_in.at[r, at, slot, rows, lanes],
+            send_sem=a_send.at[r, v, d, pc, hh], recv_sem=a_recv.at[r, at, d, pc, hh],
+            device_id=(ahead if last else s, to_peer(d)), device_id_type=MESH)
 
     def m_copy(d, landing=False):
         slot = from_peer(d) if landing else f
@@ -81,13 +88,30 @@
             device_id=(s, to_peer(d)), device_id_type=MESH)
 
     def s_copy(r, v, pc, landing=False):
-        at = v if landing else lax.rem(v + jnp.where(s == segments - 1, 1, 0), virtual)
-        target = out if r == ROUNDS - 1 else st_in.at[r]
+        at = v if landing else onward(v)
         rows = pl.ds(pc * half, half)
         return pltpu.make_async_remote_copy(
-            src_ref=st_out.at[r, v, rows], dst_ref=target.at[at, rows],
+            src_ref=st_out.at[r, v, rows], dst_ref=st_in.at[r, at, rows],
             send_sem=s_send.at[r, v, pc], recv_sem=s_recv.at[r, at, pc],
             device_id=(ahead, f), device_id_type=MESH)
+
+    def forward_copy(v, pc, landing=False):
+        at = v if landing else onward(v)
+        rows = pl.ds(pc * half, half)
+        return pltpu.make_async_remote_copy(
+            src_ref=st_in.at[ROUNDS - 2, v, rows], dst_ref=st_ahead.at[at, rows],
+            send_sem=s_send.at[ROUNDS - 1, v, pc], recv_sem=s_recv.at[ROUNDS - 1, at, pc],
+            device_id=(ahead, f), device_id_type=MESH)
+
+    def w_copy():
+        return pltpu.make_async_remote_copy(
+            src_ref=wm_all, dst_ref=wm_behind, send_sem=w_send.at[0], recv_sem=w_recv.at[0],
+            device_id=(ahead, f), device_id_type=MESH)
+
+    def store(v, pc):
+        rows = pl.ds(pc * half, half)
+        return pltpu.make_async_copy(
+            st_out.at[ROUNDS - 1, v, rows], out.at[v, rows], store_sem.at[v, pc])
 
     def state_of(r):
         return stream if r == 0 else st_in.at[r - 1]
@@ -168,29 +192,30 @@
         lax.fori_loop(0, part // step, body, 0)
 
     def pack_mix():
+        on = [jnp.where(live[v] > 0, 1.0, 0.0).astype(F32) for v in range(virtual)]
+
         def body(i, carry):
             rows = pl.ds(pl.multiple_of(i * LANES, LANES), LANES)
-            both = [wm[v, rows, :].astype(F32) for v in range(virtual)]
+            both = [wm[v, rows, :].astype(F32) * on[v] for v in range(virtual)]
             wm_all[f, rows, :] = jnp.concatenate(both, axis=1).astype(BF16)
             return carry
 
         lax.fori_loop(0, heads * heads // LANES, body, 0)
 
-    def spread_mix():
+    def spread_mix(packed, spread, place):
         def body(i, carry):
             rows = pl.ds(pl.multiple_of(i * LANES, LANES), LANES)
-            each = [wm_all[j, rows, :].astype(F32) for j in range(peers)]
+            each = [packed[j, rows, :].astype(F32) for j in range(peers)]
             for v in range(virtual):
-                wm_t[v, rows, :] = jnp.concatenate(
+                spread[place(v), rows, :] = jnp.concatenate(
                     [e[:, v * local:(v + 1) * local] for e in each], axis=1)
             return carry
 
         lax.fori_loop(0, heads * heads // LANES, body, 0)
 
     def mix(r, v, pc):
-        state = state_of(r)
-        on = jnp.full((half, hs), live[v].astype(F32))
-
+        last = r == ROUNDS - 1
+        state, maps = (st_ahead, wm_last) if last else (state_of(r), wm_t)
         rows = pl.ds(pc * half, half)
 
         def body(group, carry):
@@ -198,14 +223,13 @@
             for h in range(heads):
                 j, at = h // local_heads, (h % local_heads) * hs
                 a = att_in[r, v, j, rows, at:at + hs].astype(F32)
-                w = wm_t[v, pl.ds(pl.multiple_of(h * heads + group * 8, 8), 8), :]
+                w = maps[v, pl.ds(pl.multiple_of(h * heads + group * 8, 8), 8), :]
                 for g in range(8):
                     sums[g] = sums[g] + a * w[g:g + 1]
             for g in range(8):
                 lanes = pl.ds(pl.multiple_of((group * 8 + g) * hs, hs), hs)
                 wide = state[v, rows, lanes].astype(F32)
-                updated = wide + sums[g].astype(BF16).astype(F32)
-                st_out[r, v, rows, lanes] = jnp.where(on > 0.0, updated, wide).astype(BF16)
+                st_out[r, v, rows, lanes] = (wide + sums[g].astype(BF16).astype(F32)).astype(BF16)
             return carry
 
         lax.fori_loop(0, heads // 8, body, 0)
@@ -217,9 +241,12 @@
             for d in others:
                 x_copy(r, v, d, pc, hh).start()
 
+    def receivers(r):
+        return range(peers) if r == ROUNDS - 1 else others
+
     def send_a(r, v, hh):
         for pc in pieces:
-            for d in others:
+            for d in receivers(r):
                 a_copy(r, v, d, pc, hh).start()
 
     def wait_x(r, v, hh):
@@ -228,11 +255,12 @@
                 x_copy(r, v, d, pc, hh, landing=True).wait_recv()
 
     def wait_a(r, v, pc):
-        for d in others:
+        for d in receivers(r):
             for hh in pieces:
                 a_copy(r, v, d, pc, hh, landing=True).wait_recv()
 
     for r in range(ROUNDS):
+        last = r == ROUNDS - 1
         todo = order(r)
         for o, v in enumerate(todo):
             if r == 0:
@@ -243,9 +271,11 @@
                     s_copy(r - 1, v, pc, landing=True).wait_recv()
                 norm(r, v, pc)
                 if r == 0 and o == 0 and pc == 0:
-                    pl.semaphore_wait(barrier, peers + 1)
+                    pl.semaphore_wait(barrier, everyone)
                 if o == 0:
                     send_x(r, v, pc)
+                if last:
+                    forward_copy(v, pc).start()
             gath[r, v, f] = xn[r, v, f]
         if r == 0:
             pack_mix()
@@ -264,35 +294,50 @@
                         for d in others:
                             m_copy(d).start()
                 attention(r, v, hh)
-                if o == 0:
+                if o == 0 or last:
                     send_a(r, v, hh)
-            att_in[r, v, f] = att_out[r, v, f]
+            if not last:
+                att_in[r, v, f] = att_out[r, v, f]
         if r == 0:
             for d in others:
                 m_copy(d, landing=True).wait_recv()
-            spread_mix()
-        for o, v in enumerate(todo):
+            w_copy().start()
+            spread_mix(wm_all, wm_t, lambda v: v)
+        if last:
+            w_copy().wait_recv()
+            spread_mix(wm_behind, wm_last, lambda v: lax.rem(v + jnp.where(s == 0, 1, 0), virtual))
+        done = order(r + 1) if last else todo
+        for o, v in enumerate(done):
             for pc in pieces:
                 wait_a(r, v, pc)
-                if pc == 0 and o + 1 < virtual:
+                if last:
+                    forward_copy(v, pc, landing=True).wait_recv()
+                elif pc == 0 and o + 1 < virtual:
                     for hh in pieces:
-                        send_a(r, todo[o + 1], hh)
+                        send_a(r, done[o + 1], hh)
                 mix(r, v, pc)
-                s_copy(r, v, pc).start()
-
-    for v in range(virtual):
-        for pc in pieces:
-            s_copy(ROUNDS - 1, v, pc, landing=True).wait_recv()
+                if last:
+                    store(v, pc).start()
+                else:
+                    s_copy(r, v, pc).start()
+
     for r in range(ROUNDS):
+        last = r == ROUNDS - 1
         for v in range(virtual):
             for pc in pieces:
-                for d in others:
-                    for hh in pieces:
+                for hh in pieces:
+                    for d in others:
                         x_copy(r, v, d, pc, hh).wait_send()
+                    for d in receivers(r):
                         a_copy(r, v, d, pc, hh).wait_send()
-                s_copy(r, v, pc).wait_send()
+                if last:
+                    forward_copy(v, pc).wait_send()
+                    store(v, pc).wait()
+                else:
+                    s_copy(r, v, pc).wait_send()
     for d in others:
         m_copy(d).wait_send()
+    w_copy().wait_send()
 
 
 def shards(segments, peers, stream, gain, w_query, w_key, w_value, w_mix, active, random_blocks):
@@ -327,15 +372,21 @@
             pltpu.VMEM((peers, heads * heads, virtual * local), BF16),
             pltpu.VMEM((virtual, heads * heads, hs), F32),
             pltpu.VMEM((virtual, seq, seq), F32),
+            pltpu.VMEM((virtual, tokens, width), BF16),
+            pltpu.VMEM((peers, heads * heads, virtual * local), BF16),
+            pltpu.VMEM((virtual, heads * heads, hs), F32),
             dma((ROUNDS, virtual, apart, PIECES, PIECES)),
             dma((ROUNDS, virtual, apart, PIECES, PIECES)),
-            dma((ROUNDS, virtual, apart, PIECES, PIECES)),
-            dma((ROUNDS, virtual, apart, PIECES, PIECES)),
+            dma((ROUNDS, virtual, peers, PIECES, PIECES)),
+            dma((ROUNDS, virtual, peers, PIECES, PIECES)),
             dma((ROUNDS, virtual, PIECES)),
             dma((ROUNDS, virtual, PIECES)),
             dma((apart,)),
             dma((apart,)),
             dma((4, virtual)),
+            dma((1,)),
+            dma((1,)),
+            dma((virtual, PIECES)),
         ],
         compiler_params=pltpu.CompilerParams(
             collective_id=0, has_side_effects=True, vmem_limit_bytes=56 * 1024 * 1024

time: 71.1 us -> 71.5 us (level)
  no operation moved by 1% of the time
where the time goes in v5:
time: 71.5 us; the launch traced here: 71.3 us
  Pallas kernels  69 us (97%)
  local copies, waits for them, and re-layouts  2.29 us (3%)
    pallas_call x1, Pallas kernels, shards(): pl.pallas_call(functools.partial(kernel, segments, peers), out_shape=jax....  69 us
    unnamed x1, local copies, waits for them, and re-layouts  2.29 us

profile of v5, /device:TPU:0, one launch (start us, length us, event | category | flops | bytes accessed | tf_op | source)
XLA Modules:
  0.0 71.3 jit_solution(1329091605919110546)
XLA Ops:
  0.0 69.0 %shard_map.82 = bf16[2,64,4096]{2,1,0:T(8,128)(2,1)} custom-call(bf16[2,64,4096]{2,1,0:T(8,128)(2,1)} %bitcast.16, bf16[2,4096]{1,0:T(2,128)(2,1)} %bitcast.21, bf16[2,16,128,128]{3,2,1,0:T(8,128)(2,1)} %bitcast.17, bf16[2,16,128,128]{3,2,1,0:T(8,128)(2,1)} %bitcast.18, bf16[2,16,128,128]{3,2,1,0:T(8,128)(2,1)} %bitcast.19, bf16[2,1024,64]{2,1,0:T(8,128)(2,1)} %bitcast.20, ...), custom_call_target="tpu_custom_call" | custom-call | flops 1342177280 | bytes 6291456 | tf_op jit(solution)/shard_map/pallas_call | solution.py:355
  69.0 2.3 %copy.11 = bf16[2,1,64,4096]{3,2,1,0:T(8,128)(2,1)} copy(bf16[2,1,64,4096]{3,2,1,0:T(8,128)(2,1)} %bitcast.15) | data formatting | bytes 2097152

commit v6 on v4

--- a/solution.py
+++ b/solution.py
@@ -12,6 +12,7 @@
 EPS = 1e-05
 LANES = 128
 PIECES = 2
+GROUPS = 4
 MESH = pl.DeviceIdType.MESH
 F32 = jnp.float32
 BF16 = jnp.bfloat16
@@ -26,7 +27,7 @@
     virtual, tokens, width = stream.shape
     local_heads, hs = wq.shape[1], wq.shape[2]
     half = tokens // PIECES
-    part = local_heads // PIECES
+    part = local_heads // GROUPS
     local = wm.shape[2]
     heads = width // hs
     seq = tokens * peers
@@ -80,13 +81,13 @@
             send_sem=m_send.at[d - 1], recv_sem=m_recv.at[d - 1],
             device_id=(s, to_peer(d)), device_id_type=MESH)
 
-    def s_copy(r, v, pc, landing=False):
+    def s_copy(r, v, pc, side, landing=False):
         at = v if landing else lax.rem(v + jnp.where(s == segments - 1, 1, 0), virtual)
         target = out if r == ROUNDS - 1 else st_in.at[r]
-        rows = pl.ds(pc * half, half)
+        rows, lanes = pl.ds(pc * half, half), pl.ds(side * (width // 2), width // 2)
         return pltpu.make_async_remote_copy(
-            src_ref=st_out.at[r, v, rows], dst_ref=target.at[at, rows],
-            send_sem=s_send.at[r, v, pc], recv_sem=s_recv.at[r, at, pc],
+            src_ref=st_out.at[r, v, rows, lanes], dst_ref=target.at[at, rows, lanes],
+            send_sem=s_send.at[r, v, pc, side], recv_sem=s_recv.at[r, at, pc, side],
             device_id=(ahead, f), device_id_type=MESH)
 
     def state_of(r):
@@ -187,7 +188,7 @@
 
         lax.fori_loop(0, heads * heads // LANES, body, 0)
 
-    def mix(r, v, pc):
+    def mix(r, v, pc, side):
         state = state_of(r)
         on = jnp.full((half, hs), live[v].astype(F32))
 
@@ -208,14 +209,16 @@
                 st_out[r, v, rows, lanes] = jnp.where(on > 0.0, updated, wide).astype(BF16)
             return carry
 
-        lax.fori_loop(0, heads // 8, body, 0)
+        lax.fori_loop(side * (heads // 16), (side + 1) * (heads // 16), body, 0)
 
     others = range(1, peers)
     pieces = range(PIECES)
-    def send_x(r, v, pc):
-        for hh in pieces:
-            for d in others:
-                x_copy(r, v, d, pc, hh).start()
+    groups = range(GROUPS)
+    sides = range(2)
+
+    def send_x(r, v, pc, hh):
+        for d in others:
+            x_copy(r, v, d, pc, hh).start()
 
     def send_a(r, v, hh):
         for pc in pieces:
@@ -229,7 +232,7 @@
 
     def wait_a(r, v, pc):
         for d in others:
-            for hh in pieces:
+            for hh in groups:
                 a_copy(r, v, d, pc, hh, landing=True).wait_recv()
 
     for r in range(ROUNDS):
@@ -240,12 +243,17 @@
                 gain[v] = gain_in[v:v + 1, :].astype(F32)
             for pc in pieces:
                 if r > 0:
-                    s_copy(r - 1, v, pc, landing=True).wait_recv()
+                    for side in sides:
+                        s_copy(r - 1, v, pc, side, landing=True).wait_recv()
                 norm(r, v, pc)
-                if r == 0 and o == 0 and pc == 0:
-                    pl.semaphore_wait(barrier, peers + 1)
-                if o == 0:
-                    send_x(r, v, pc)
+                if r > 0 and o == 0:
+                    for hh in groups:
+                        send_x(r, v, pc, hh)
+            if r == 0 and o == 0:
+                pl.semaphore_wait(barrier, peers + 1)
+                for hh in groups:
+                    for pc in pieces:
+                        send_x(r, v, pc, hh)
             gath[r, v, f] = xn[r, v, f]
         if r == 0:
             pack_mix()
@@ -254,45 +262,60 @@
             if r == 0:
                 for n in range(1, 4):
                     load(n, v).wait()
-            for hh in pieces:
+            for hh in groups:
                 wait_x(r, v, hh)
-                if hh == 0:
-                    if o + 1 < virtual:
-                        for pc in pieces:
-                            send_x(r, todo[o + 1], pc)
-                    if r == 0 and o == 0:
-                        for d in others:
-                            m_copy(d).start()
+                if o + 1 < virtual:
+                    for pc in pieces:
+                        send_x(r, todo[o + 1], pc, hh)
+                if r == 0 and o == 0 and hh == GROUPS - 1:
+                    for d in others:
+                        m_copy(d).start()
                 attention(r, v, hh)
-                if o == 0:
-                    send_a(r, v, hh)
+                send_a(r, v, hh)
             att_in[r, v, f] = att_out[r, v, f]
         if r == 0:
             for d in others:
                 m_copy(d, landing=True).wait_recv()
             spread_mix()
-        for o, v in enumerate(todo):
+        for v in todo:
             for pc in pieces:
                 wait_a(r, v, pc)
-                if pc == 0 and o + 1 < virtual:
-                    for hh in pieces:
-                        send_a(r, todo[o + 1], hh)
-                mix(r, v, pc)
-                s_copy(r, v, pc).start()
+                for side in sides:
+                    mix(r, v, pc, side)
+                    s_copy(r, v, pc, side).start()
 
     for v in range(virtual):
         for pc in pieces:
-            s_copy(ROUNDS - 1, v, pc, landing=True).wait_recv()
+            for side in sides:
+                s_copy(ROUNDS - 1, v, pc, side, landing=True).wait_recv()
     for r in range(ROUNDS):
         for v in range(virtual):
             for pc in pieces:
                 for d in others:
-                    for hh in pieces:
+                    for hh in groups:
                         x_copy(r, v, d, pc, hh).wait_send()
                         a_copy(r, v, d, pc, hh).wait_send()
-                s_copy(r, v, pc).wait_send()
+                for side in sides:
+                    s_copy(r, v, pc, side).wait_send()
     for d in others:
         m_copy(d).wait_send()
+
+
+def copy_kernel(source, target, sem):
+    virtual, tokens, _ = source.shape
+    count = sem.shape[1]
+    step = tokens // count
+
+    def piece(v, i):
+        rows = pl.ds(i * step, step)
+        return pltpu.make_async_copy(source.at[v, rows], target.at[v, rows], sem.at[v, i])
+
+    for v in range(virtual):
+        for i in range(count):
+            piece(v, i).start()
+    for v in range(virtual):
+        for i in range(count):
+            piece(v, i).wait()
 
 
 def shards(segments, peers, stream, gain, w_query, w_key, w_value, w_mix, active, random_blocks):
@@ -327,12 +350,12 @@
             pltpu.VMEM((peers, heads * heads, virtual * local), BF16),
             pltpu.VMEM((virtual, heads * heads, hs), F32),
             pltpu.VMEM((virtual, seq, seq), F32),
-            dma((ROUNDS, virtual, apart, PIECES, PIECES)),
-            dma((ROUNDS, virtual, apart, PIECES, PIECES)),
-            dma((ROUNDS, virtual, apart, PIECES, PIECES)),
-            dma((ROUNDS, virtual, apart, PIECES, PIECES)),
-            dma((ROUNDS, virtual, PIECES)),
-            dma((ROUNDS, virtual, PIECES)),
+            dma((ROUNDS, virtual, apart, PIECES, GROUPS)),
+            dma((ROUNDS, virtual, apart, PIECES, GROUPS)),
+            dma((ROUNDS, virtual, apart, PIECES, GROUPS)),
+            dma((ROUNDS, virtual, apart, PIECES, GROUPS)),
+            dma((ROUNDS, virtual, PIECES, 2)),
+            dma((ROUNDS, virtual, PIECES, 2)),
             dma((apart,)),
             dma((apart,)),
             dma((4, virtual)),
@@ -355,7 +378,16 @@
         active[:, 0],
         random_blocks[:, 0],
     )
-    return result[:, None]
+    written = pl.pallas_call(
+        copy_kernel,
+        out_shape=jax.ShapeDtypeStruct(result.shape, BF16),
+        in_specs=[hbm],
+        out_specs=hbm,
+        scratch_shapes=[dma((virtual, 4))],
+        compiler_params=pltpu.CompilerParams(vmem_limit_bytes=60 * 1024 * 1024),
+        cost_estimate=pl.CostEstimate(flops=0, bytes_accessed=4 * virtual * tokens * width, transcendentals=0),
+    )(result)
+    return written[:, None]
 
 
 def solution(mesh):

time: 71.1 us -> 103 us (1.45)
  Pallas kernels: 68.6 us -> 103 us
  local copies, waits for them, and re-layouts: 2.29 us -> 0 us
    pallas_call x0 -> x1, Pallas kernels: none -> 32.9 us  [shards(): pl.pallas_call(copy_kernel, out_shape=jax.ShapeDtypeStruct(result.shape,...]
    unnamed x1 -> x0, local copies, waits for them, and re-layouts: 2.29 us -> none
    pallas_call x1, Pallas kernels: 68.6 us -> 70 us  [shards(): pl.pallas_call(functools.partial(kernel, segments, peers), out_shape=jax....]
where the time goes in v6:
time: 103 us
  Pallas kernels  103 us (100%)
    pallas_call x1, Pallas kernels, shards(): pl.pallas_call(functools.partial(kernel, segments, peers), out_shape=jax....  70 us
    pallas_call x1, Pallas kernels, shards(): pl.pallas_call(copy_kernel, out_shape=jax.ShapeDtypeStruct(result.shape,...  32.9 us

profile of v6, /device:TPU:0, one launch (start us, length us, event | category | flops | bytes accessed | tf_op | source)
XLA Modules:
  0.0 103.0 jit_solution(17070415497229857150)
XLA Ops:
  0.0 70.0 %shard_map.82.source = bf16[2,64,4096]{2,1,0:T(8,128)(2,1)} custom-call(bf16[2,64,4096]{2,1,0:T(8,128)(2,1)} %bitcast.15, bf16[2,4096]{1,0:T(2,128)(2,1)} %bitcast.20, bf16[2,16,128,128]{3,2,1,0:T(8,128)(2,1)} %bitcast.16, bf16[2,16,128,128]{3,2,1,0:T(8,128)(2,1)} %bitcast.17, bf16[2,16,128,128]{3,2,1,0:T(8,128)(2,1)} %bitcast.18, ...), custom_call_target="tpu_custom_call" | custom-call | flops 1342177280 | bytes 6291456 | tf_op jit(solution)/shard_map/pallas_call | solution.py:333
  70.0 32.9 %shard_map.83 = bf16[2,64,4096]{2,1,0:T(8,128)(2,1)} custom-call(bf16[2,64,4096]{2,1,0:T(8,128)(2,1)} %shard_map.82.source), custom_call_target="tpu_custom_call" | custom-call | bytes 2097152 | tf_op jit(solution)/shard_map/pallas_call | solution.py:381

commit v7 on v4

--- a/solution.py
+++ b/solution.py
@@ -293,6 +293,10 @@
                 s_copy(r, v, pc).wait_send()
     for d in others:
         m_copy(d).wait_send()
+
+
+def copy_kernel(source, target):
+    target[...] = source[...]
 
 
 def shards(segments, peers, stream, gain, w_query, w_key, w_value, w_mix, active, random_blocks):
@@ -355,7 +359,16 @@
         active[:, 0],
         random_blocks[:, 0],
     )
-    return result[:, None]
+    block = pl.BlockSpec((1, tokens // PIECES, width), lambda v, i: (v, i, 0))
+    written = pl.pallas_call(
+        copy_kernel,
+        grid=(virtual, PIECES),
+        out_shape=jax.ShapeDtypeStruct(result.shape, BF16),
+        in_specs=[block],
+        out_specs=block,
+        compiler_params=pltpu.CompilerParams(vmem_limit_bytes=60 * 1024 * 1024),
+    )(result)
+    return written[:, None]
 
 
 def solution(mesh):

time: 71.1 us -> 72.2 us (1.015)
  Pallas kernels: 68.6 us -> 72 us
  local copies, waits for them, and re-layouts: 2.29 us -> 0 us
    pallas_call x0 -> x1, Pallas kernels: none -> 3.37 us  [shards(): pl.pallas_call(copy_kernel, grid=(virtual, PIECES), out_shape=jax.ShapeDt...]
    unnamed x1 -> x0, local copies, waits for them, and re-layouts: 2.29 us -> none
where the time goes in v7:
time: 72.2 us; the launch traced here: 72 us
  Pallas kernels  72 us (100%)
    pallas_call x1, Pallas kernels, shards(): pl.pallas_call(functools.partial(kernel, segments, peers), out_shape=jax....  68.6 us
    pallas_call x1, Pallas kernels, shards(): pl.pallas_call(copy_kernel, grid=(virtual, PIECES), out_shape=jax.ShapeDt...  3.37 us

profile of v7, /device:TPU:0, one launch (start us, length us, event | category | flops | bytes accessed | tf_op | source)
XLA Modules:
  0.0 72.0 jit_solution(18148385871086520474)
XLA Ops:
  0.0 68.6 %shard_map.82.source = bf16[2,64,4096]{2,1,0:T(8,128)(2,1)} custom-call(bf16[2,64,4096]{2,1,0:T(8,128)(2,1)} %bitcast.15, bf16[2,4096]{1,0:T(2,128)(2,1)} %bitcast.20, bf16[2,16,128,128]{3,2,1,0:T(8,128)(2,1)} %bitcast.16, bf16[2,16,128,128]{3,2,1,0:T(8,128)(2,1)} %bitcast.17, bf16[2,16,128,128]{3,2,1,0:T(8,128)(2,1)} %bitcast.18, ...), custom_call_target="tpu_custom_call" | custom-call | flops 1342177280 | bytes 6291456 | tf_op jit(solution)/shard_map/pallas_call | solution.py:314
  68.6 3.4 %shard_map.83 = bf16[2,64,4096]{2,1,0:T(8,128)(2,1)} custom-call(bf16[2,64,4096]{2,1,0:T(8,128)(2,1)} %shard_map.82.source), custom_call_target="tpu_custom_call" | custom-call | tf_op jit(solution)/shard_map/pallas_call | solution.py:363
